TPU v7x, 512 devices: a whole 4x4x16 slice. The times are simulated.
512 devices in a mesh: dp: 16 (over z_lo, core), ctx: 32 (over y, x, z_hi).
Axes of the slice: x: 4, y: 4, z: 16 (z_hi: 2, z_lo: 8; z = z_hi * 8 + z_lo), core: 2. Of those that a mesh axis runs over, the one named last changes fastest.
Arguments:
- value: bfloat16 [16384, 8192], P('ctx', 'dp'), may hold values from -6 to 6
- gate: bfloat16 [16384, 8192], P('ctx', 'dp'), may hold values from -6 to 6
- grad_out: bfloat16 [16384, 8192], P('ctx', 'dp'), may hold values from -6 to 6
- filter_taps: float32 [16384, 32, 16], P('dp', 'ctx'), may hold values from -4 to 4
- skip: float32 [8192], P('dp'), may hold values from -3 to 3
Outputs:
- gate_grad: bfloat16 [16384, 8192], P('ctx', 'dp')
- filter_grad: float32 [16384, 32, 16], P('dp', 'ctx')
All inputs are finite; a program needn't handle non-finite values.
Results may differ from a plain program's by a relative error of at most 0.012.
Values may be sent and summed in bfloat16 or wider, within the bound.
A program may use at most 64 MiB of HBM per device.

v0:
```python
import math

import jax
import jax.numpy as jnp
from jax import lax
from jax.sharding import PartitionSpec as P

GROUP = 16


def split_length(padded_length):
    factor_low = math.isqrt(padded_length)
    while factor_low > 1 and (
        padded_length % factor_low != 0 or padded_length // factor_low % 2 != 0
    ):
        factor_low = factor_low - 1
    return (padded_length // factor_low, factor_low)


def phase_grid(row_count, col_count, period):
    row_ids = jnp.arange(row_count, dtype=jnp.int32)[:, None]
    col_ids = jnp.arange(col_count, dtype=jnp.int32)[None, :]
    reduced = row_ids * col_ids % period
    return reduced.astype(jnp.float32) * (2.0 * math.pi / period)


def contract(form, table, operand):
    return jnp.einsum(form, table, operand, precision=lax.Precision.HIGHEST)


def forward_real(signal, factor_high, factor_low):
    half_rows = factor_high // 2
    count = signal.shape[0]
    shaped = signal.reshape(count, half_rows, factor_low)
    angles_first = phase_grid(factor_high, half_rows, factor_high)
    first_re = contract("kt,wtb->wkb", jnp.cos(angles_first), shaped)
    first_im = -contract("kt,wtb->wkb", jnp.sin(angles_first), shaped)
    twist = phase_grid(factor_high, factor_low, factor_high * factor_low)[None, :, :]
    twist_cos = jnp.cos(twist)
    twist_sin = jnp.sin(twist)
    turned_re = first_re * twist_cos + first_im * twist_sin
    turned_im = first_im * twist_cos - first_re * twist_sin
    angles_second = phase_grid(factor_low, factor_low, factor_low)
    second_cos = jnp.cos(angles_second)
    second_sin = jnp.sin(angles_second)
    out_re = contract("qb,wkb->wkq", second_cos, turned_re) + contract(
        "qb,wkb->wkq", second_sin, turned_im
    )
    out_im = contract("qb,wkb->wkq", second_cos, turned_im) - contract(
        "qb,wkb->wkq", second_sin, turned_re
    )
    return (out_re, out_im)


def inverse_pair(spec_re, spec_im, factor_high, factor_low):
    half_rows = factor_high // 2
    count = spec_re.shape[0]
    angles_second = phase_grid(factor_low, factor_low, factor_low)
    second_cos = jnp.cos(angles_second)
    second_sin = jnp.sin(angles_second)
    middle_re = contract("bq,wkq->wkb", second_cos, spec_re) - contract(
        "bq,wkq->wkb", second_sin, spec_im
    )
    middle_im = contract("bq,wkq->wkb", second_sin, spec_re) + contract(
        "bq,wkq->wkb", second_cos, spec_im
    )
    twist = phase_grid(factor_high, factor_low, factor_high * factor_low)[None, :, :]
    twist_cos = jnp.cos(twist)
    twist_sin = jnp.sin(twist)
    turned_re = middle_re * twist_cos - middle_im * twist_sin
    turned_im = middle_re * twist_sin + middle_im * twist_cos
    angles_first = phase_grid(half_rows, factor_high, factor_high)
    first_cos = jnp.cos(angles_first)
    first_sin = jnp.sin(angles_first)
    real_part = contract("tk,wkb->wtb", first_cos, turned_re) - contract(
        "tk,wkb->wtb", first_sin, turned_im
    )
    imag_part = contract("tk,wkb->wtb", first_sin, turned_re) + contract(
        "tk,wkb->wtb", first_cos, turned_im
    )
    scaling = 1.0 / (factor_high * factor_low)
    real_part = real_part.reshape(count, half_rows * factor_low) * scaling
    imag_part = imag_part.reshape(count, half_rows * factor_low) * scaling
    return (real_part, imag_part)


def shards(value, gate, grad_out, filter_taps, skip):
    value_cols, gate_cols, cotangent_cols = (
        lax.all_to_all(value.T, "ctx", split_axis=0, concat_axis=1, tiled=True),
        lax.all_to_all(gate.T, "ctx", split_axis=0, concat_axis=1, tiled=True),
        lax.all_to_all(grad_out.T, "ctx", split_axis=0, concat_axis=1, tiled=True),
    )
    gated_cols = (gate_cols.astype(jnp.float32) * cotangent_cols.astype(jnp.float32)).astype(
        jnp.bfloat16
    )
    taps_cols = lax.all_to_all(filter_taps, "dp", split_axis=2, concat_axis=0, tiled=True)
    group_taps = taps_cols[:, :, 0].T
    channels_dev = value_cols.shape[0]
    length = value_cols.shape[1]
    value_wide = value_cols.astype(jnp.float32)
    factor_high, factor_low = split_length(2 * length)
    filter_time = group_taps / jnp.sqrt(jnp.float32(length))
    filter_re, filter_im = forward_real(filter_time, factor_high, factor_low)
    filter_re = jnp.repeat(filter_re, GROUP, axis=0)
    filter_im = jnp.repeat(filter_im, GROUP, axis=0)
    value_re, value_im = forward_real(value_wide, factor_high, factor_low)
    gated_re, gated_im = forward_real(gated_cols.astype(jnp.float32), factor_high, factor_low)
    conv_re = value_re * filter_re - value_im * filter_im
    conv_im = value_re * filter_im + value_im * filter_re
    corr_re = gated_re * value_re + gated_im * value_im
    corr_im = gated_im * value_re - gated_re * value_im
    conv, corr = inverse_pair(conv_re - corr_im, conv_im + corr_re, factor_high, factor_low)
    skip_dev = lax.dynamic_slice_in_dim(skip, lax.axis_index("ctx") * channels_dev, channels_dev)
    long_out = (conv + skip_dev[:, None] * value_wide).astype(jnp.bfloat16)
    grads_cols = (cotangent_cols.astype(jnp.float32) * long_out.astype(jnp.float32)).astype(
        jnp.bfloat16
    )
    gate_grad = lax.all_to_all(grads_cols, "ctx", split_axis=1, concat_axis=0, tiled=True).T
    grouped = jnp.sum(corr.reshape(channels_dev // GROUP, GROUP, length), axis=1)
    scaled = grouped / jnp.sqrt(jnp.float32(length * GROUP))
    filter_grad = lax.all_to_all(
        scaled.T[:, :, None].astype(jnp.bfloat16), "dp", split_axis=0, concat_axis=2, tiled=True
    ).astype(jnp.float32)
    return (gate_grad, filter_grad)


def solution(mesh):
    in_specs = (P("ctx", "dp"), P("ctx", "dp"), P("ctx", "dp"), P("dp", "ctx", None), P("dp"))
    out_specs = (P("ctx", "dp"), P("dp", "ctx", None))
    return jax.shard_map(shards, mesh=mesh, in_specs=in_specs, out_specs=out_specs, check_vma=False)
```

profile of v0, /device:TPU:33, one launch (start us, length us, event | category | flops | bytes accessed | tf_op | source)
XLA Modules:
  0.0 384.7 jit_solution(7216258013057969965)
XLA Ops:
  0.6 1.6 copy.66
  2.2 13.0 %all-to-all-start.2 = ((f32[1024,1,16]{0,1,2:T(1,128)}), f32[1024,1,16]{0,1,2:T(1,128)S(1)}, u32[]{:S(2)}, u32[]{:S(2)}) async-start(f32[1024,1,16]{0,1,2:T(1,128)} %copy.66), calls=%async_computation.2 | async-start | bytes 131072 | tf_op jit(solution)/shard_map/all_to_all | solution.py:96
  15.2 2.0 copy.67
  17.2 7.0 %all-to-all-done.2 = f32[1024,1,16]{0,1,2:T(1,128)S(1)} async-done(((f32[1024,1,16]{0,1,2:T(1,128)}), f32[1024,1,16]{0,1,2:T(1,128)S(1)}, u32[]{:S(2)}, u32[]{:S(2)}) %all-to-all-start.2) | async-done | bytes 65568 | tf_op jit(solution)/shard_map/all_to_all | solution.py:96
  24.2 12.8 %all-to-all-start.3 = ((bf16[32,16,512]{2,1,0:T(8,128)(2,1)}), bf16[32,16,512]{2,1,0:T(8,128)(2,1)S(1)}, u32[]{:S(2)}, u32[]{:S(2)}) async-start(bf16[32,16,512]{2,1,0:T(8,128)(2,1)} %bitcast.26), calls=%async_computation.3 | async-start | bytes 1048576 | tf_op jit(solution)/shard_map/all_to_all | solution.py:90
  37.0 0.0 copy-done.4
  37.0 1.0 copy.63
  38.0 37.0 %all-to-all-done.3 = bf16[32,16,512]{2,1,0:T(8,128)(2,1)S(1)} async-done(((bf16[32,16,512]{2,1,0:T(8,128)(2,1)}), bf16[32,16,512]{2,1,0:T(8,128)(2,1)S(1)}, u32[]{:S(2)}, u32[]{:S(2)}) %all-to-all-start.3) | async-done | bytes 524320 | tf_op jit(solution)/shard_map/all_to_all | solution.py:90
  75.1 3.9 %all-to-all-start = ((bf16[32,16,512]{2,1,0:T(8,128)(2,1)}), bf16[32,16,512]{2,1,0:T(8,128)(2,1)S(1)}, u32[]{:S(2)}, u32[]{:S(2)}) async-start(bf16[32,16,512]{2,1,0:T(8,128)(2,1)} %bitcast.1), calls=%async_computation | async-start | bytes 1048576 | tf_op jit(solution)/shard_map/all_to_all | solution.py:91
  79.0 0.5 fusion.102
  79.5 0.1 copy.72
  79.6 0.1 copy.70
  79.7 1.0 copy.64
  80.7 0.8 dynamic_slice.3
  81.5 0.1 broadcast_multiply_fusion
  81.5 20.2 %all-to-all-done = bf16[32,16,512]{2,1,0:T(8,128)(2,1)S(1)} async-done(((bf16[32,16,512]{2,1,0:T(8,128)(2,1)}), bf16[32,16,512]{2,1,0:T(8,128)(2,1)S(1)}, u32[]{:S(2)}, u32[]{:S(2)}) %all-to-all-start) | async-done | bytes 524320 | tf_op jit(solution)/shard_map/all_to_all | solution.py:91
  101.7 9.1 %all-to-all-start.1 = ((bf16[32,16,512]{2,1,0:T(8,128)(2,1)}), bf16[32,16,512]{2,1,0:T(8,128)(2,1)}, u32[]{:S(2)}, u32[]{:S(2)}) async-start(bf16[32,16,512]{2,1,0:T(8,128)(2,1)} %bitcast.5), calls=%async_computation.1 | async-start | bytes 1048576 | tf_op jit(solution)/shard_map/all_to_all | solution.py:89
  110.8 0.8 convolution_bitcast_fusion
  111.6 0.8 fusion.20
  112.3 1.1 fusion.48
  113.4 1.1 fusion.52
  114.5 1.1 convolution_subtract_fusion.3
  115.6 1.1 convolution_add_fusion.3
  116.8 0.2 fusion.27
  117.0 0.3 copy.68
  117.3 0.3 convert_element_type.202
  117.6 1.5 fusion.58
  119.1 2.9 fusion.54
  121.9 8.4 %all-to-all-done.1 = bf16[32,16,512]{2,1,0:T(8,128)(2,1)} async-done(((bf16[32,16,512]{2,1,0:T(8,128)(2,1)}), bf16[32,16,512]{2,1,0:T(8,128)(2,1)}, u32[]{:S(2)}, u32[]{:S(2)}) %all-to-all-start.1) | async-done | bytes 524320 | tf_op jit(solution)/shard_map/all_to_all | solution.py:89
  130.3 2.1 copy.65
  132.4 1.4 reshape.194
  133.8 1.4 fusion.56
  135.2 1.9 fusion.60
  137.2 2.3 fusion.2
  139.4 2.3 fusion.4
  141.8 3.8 fusion.28
  145.6 4.0 %fusion.32 = f32[16,256,128]{2,1,0:T(8,128)S(1)} fusion(f32[16,128,256]{2,1,0:T(8,128)S(1)} %fusion.58, f32[16,128,256]{2,1,0:T(8,128)S(1)} %copy-done, f32[256,128]{0,1:T(8,128)S(1)} %copy.72, f32[256,128]{0,1:T(8,128)S(1)} %copy.70), kind=kOutput, calls=%fused_computation.48 | convolution fusion | flops 807632896 | bytes 6553600 | tf_op jit(solution)/shard_map/qb,wkb->wkq/dot_general | solution.py:28
  149.6 2.3 fusion.13
  151.9 2.3 fusion.10
  154.2 3.9 %convolution_add_fusion.1 = f32[16,256,128]{2,1,0:T(8,128)S(1)} fusion(f32[16,256,128]{2,1,0:T(8,128)S(1)} %fusion.28, f32[16,128,256]{2,1,0:T(8,128)S(1)} %fusion.58, f32[16,128,256]{2,1,0:T(8,128)S(1)} %copy-done, f32[256,128]{0,1:T(8,128)S(1)} %copy.72, f32[256,128]{0,1:T(8,128)S(1)} %copy.70), kind=kOutput, calls=%fused_computation.24 | convolution fusion | flops 808157184 | bytes 8650752 | tf_op jit(solution)/shard_map/qb,wkb->wkq/dot_general | solution.py:28
  158.0 4.8 %add_add_fusion = (f32[16,256,128]{2,1,0:T(8,128)S(1)}, f32[16,256,128]{2,1,0:T(8,128)S(1)}) fusion(f32[16,256,128]{2,1,0:T(8,128)S(1)} %fusion.13, f32[16,256,128]{2,1,0:T(8,128)S(1)} %convolution_add_fusion.1, f32[16,256,128]{2,1,0:T(8,128)S(1)} %fusion.10, f32[256,128]{1,0:T(8,128)S(1)} %convolution_subtract_fusion.3, ...), kind=kOutput, calls=%fused_computation.16 | convolution fusion | flops 815497216 | bytes 17301504 | tf_op jit(solution)/shard_map/qb,wkb->wkq/dot_general | solution.py:28
  162.9 2.2 fusion.78
  165.1 2.2 fusion.86
  167.4 2.3 convolution_add_fusion
  169.7 2.3 convolution_subtract_fusion
  172.0 2.8 fusion.25
  174.8 3.4 fusion.26
  178.2 2.4 fusion.19
  180.6 0.1 copy.83
  180.7 4.2 %fusion.17 = f32[16,128,128]{1,2,0:T(8,128)S(1)} fusion(f32[16,128,128]{2,1,0:T(8,128)} %fusion.26, f32[16,256,128]{1,2,0:T(8,128)S(1)} %convolution_add_fusion, f32[16,256,128]{1,2,0:T(8,128)} %copy-done.1, f32[256,128]{0,1:T(8,128)S(1)} %copy.72, f32[256,128]{0,1:T(8,128)S(1)} %copy.70), kind=kOutput, calls=%fused_computation.29 | convolution fusion | flops 807862272 | bytes 6553600 | tf_op jit(solution)/shard_map/tk,wkb->wtb/dot_general | solution.py:28
  184.9 0.3 copy.81
  185.2 0.2 mul.684
  185.4 11.3 %convert_element_type.219 = bf16[16384,1,1]{2,1,0:T(2,128)(2,1)} reshape(bf16[128,128]{1,0:T(8,128)(2,1)S(1)} %copy.83) | data formatting | bytes 65536 | tf_op jit(solution)/shard_map/convert_element_type | solution.py:122
  196.7 0.5 broadcast.402
  197.2 123.8 %reduce.2 = bf16[16384]{0:T(1024)(128)(2,1)S(1)} reduce(bf16[16384,1,1]{2,1,0:T(2,128)(2,1)} %convert_element_type.219, bf16[]{:T(256)} %broadcast.402), dimensions={1,2}, to_apply=%convert_element_type.219.reduce_sub_computation | reduce | bytes 65538 | tf_op jit(solution)/shard_map/convert_element_type | solution.py:122
  321.0 0.6 reshape.211
  321.6 9.3 %all-to-all-start.5 = ((bf16[16,2,512]{2,1,0:T(2,128)(2,1)}), bf16[16,2,512]{2,1,0:T(2,128)(2,1)S(1)}, u32[]{:S(2)}, u32[]{:S(2)}) async-start(bf16[16,2,512]{2,1,0:T(2,128)(2,1)} %reshape.211), calls=%async_computation.5 | async-start | bytes 65536 | tf_op jit(solution)/shard_map/all_to_all | solution.py:121
  330.9 2.5 fusion.22
  333.5 6.4 %all-to-all-done.5 = bf16[16,2,512]{2,1,0:T(2,128)(2,1)S(1)} async-done(((bf16[16,2,512]{2,1,0:T(2,128)(2,1)}), bf16[16,2,512]{2,1,0:T(2,128)(2,1)S(1)}, u32[]{:S(2)}, u32[]{:S(2)}) %all-to-all-start.5) | async-done | bytes 32800 | tf_op jit(solution)/shard_map/all_to_all | solution.py:121
  339.8 5.4 %all-to-all-start.4 = ((bf16[16,32,512]{2,0,1:T(8,128)(2,1)}), bf16[16,32,512]{2,0,1:T(8,128)(2,1)S(1)}, u32[]{:S(2)}, u32[]{:S(2)}) async-start(bf16[16,32,512]{2,0,1:T(8,128)(2,1)} %fusion.22), calls=%async_computation.4 | async-start | bytes 1048576 | tf_op jit(solution)/shard_map/all_to_all | solution.py:118
  345.3 11.2 %reshape.212 = bf16[16384,1,1]{2,1,0:T(2,128)(2,1)} reshape(bf16[16,2,512]{2,1,0:T(2,128)(2,1)S(1)} %all-to-all-done.5) | data formatting | bytes 65536
  356.5 11.4 %copy.85 = f32[16,1024,1,1]{1,0,3,2:T(8,128)} copy(bf16[16,1024,1,1]{3,2,1,0:T(2,128)(2,1)} %bitcast.154) | data formatting | bytes 98304 | tf_op jit(solution)/shard_map/convert_element_type | solution.py:123
  368.0 15.5 %all-to-all-done.4 = bf16[16,32,512]{2,0,1:T(8,128)(2,1)S(1)} async-done(((bf16[16,32,512]{2,0,1:T(8,128)(2,1)}), bf16[16,32,512]{2,0,1:T(8,128)(2,1)S(1)}, u32[]{:S(2)}, u32[]{:S(2)}) %all-to-all-start.4) | async-done | bytes 524320 | tf_op jit(solution)/shard_map/all_to_all | solution.py:118
  383.5 1.0 copy.86
  (12 shorter events, 0.0 us)
Async XLA Ops:
  0.6 36.4 %copy-start.4 = (bf16[512,512]{1,0:T(8,128)(2,1)S(1)}, bf16[512,512]{1,0:T(8,128)(2,1)}, u32[]{:S(2)}) copy-start(bf16[512,512]{1,0:T(8,128)(2,1)} %param.7) | copy-start | bytes 1572868
  2.2 22.0 %all-to-all-start.2 = ((f32[1024,1,16]{0,1,2:T(1,128)}), f32[1024,1,16]{0,1,2:T(1,128)S(1)}, u32[]{:S(2)}, u32[]{:S(2)}) async-start(f32[1024,1,16]{0,1,2:T(1,128)} %copy.66), calls=%async_computation.2 | async-start | bytes 131072 | tf_op jit(solution)/shard_map/all_to_all | solution.py:96
  17.2 62.5 %copy-start.5 = (bf16[512,512]{1,0:T(8,128)(2,1)S(1)}, bf16[512,512]{1,0:T(8,128)(2,1)}, u32[]{:S(2)}) copy-start(bf16[512,512]{1,0:T(8,128)(2,1)} %param.5) | copy-start | bytes 1572868
  24.2 50.8 %all-to-all-start.3 = ((bf16[32,16,512]{2,1,0:T(8,128)(2,1)}), bf16[32,16,512]{2,1,0:T(8,128)(2,1)S(1)}, u32[]{:S(2)}, u32[]{:S(2)}) async-start(bf16[32,16,512]{2,1,0:T(8,128)(2,1)} %bitcast.26), calls=%async_computation.3 | async-start | bytes 1048576 | tf_op jit(solution)/shard_map/all_to_all | solution.py:90
  75.1 26.6 %all-to-all-start = ((bf16[32,16,512]{2,1,0:T(8,128)(2,1)}), bf16[32,16,512]{2,1,0:T(8,128)(2,1)S(1)}, u32[]{:S(2)}, u32[]{:S(2)}) async-start(bf16[32,16,512]{2,1,0:T(8,128)(2,1)} %bitcast.1), calls=%async_computation | async-start | bytes 1048576 | tf_op jit(solution)/shard_map/all_to_all | solution.py:91
  101.7 15.1 %copy-start.2 = (bf16[32,16,512]{2,1,0:T(8,128)(2,1)}, bf16[32,16,512]{2,1,0:T(8,128)(2,1)S(1)}, u32[]{:S(2)}) copy-start(bf16[32,16,512]{2,1,0:T(8,128)(2,1)S(1)} %all-to-all-done) | copy-start | bytes 1572868
  101.7 28.6 %all-to-all-start.1 = ((bf16[32,16,512]{2,1,0:T(8,128)(2,1)}), bf16[32,16,512]{2,1,0:T(8,128)(2,1)}, u32[]{:S(2)}, u32[]{:S(2)}) async-start(bf16[32,16,512]{2,1,0:T(8,128)(2,1)} %bitcast.5), calls=%async_computation.1 | async-start | bytes 1048576 | tf_op jit(solution)/shard_map/all_to_all | solution.py:89
  139.4 2.3 copy-start
  172.0 6.2 %copy-start.1 = (f32[16,256,128]{1,2,0:T(8,128)}, f32[16,256,128]{1,2,0:T(8,128)S(1)}, u32[]{:S(2)}) copy-start(f32[16,256,128]{1,2,0:T(8,128)S(1)} %convolution_subtract_fusion) | copy-start | bytes 6291460
  197.2 133.7 %copy-start.3 = (bf16[32,16,512]{2,1,0:T(8,128)(2,1)S(1)}, bf16[32,16,512]{2,1,0:T(8,128)(2,1)}, u32[]{:S(2)}) copy-start(bf16[32,16,512]{2,1,0:T(8,128)(2,1)} %copy-done.2) | copy-start | bytes 1572868
  321.6 18.2 %all-to-all-start.5 = ((bf16[16,2,512]{2,1,0:T(2,128)(2,1)}), bf16[16,2,512]{2,1,0:T(2,128)(2,1)S(1)}, u32[]{:S(2)}, u32[]{:S(2)}) async-start(bf16[16,2,512]{2,1,0:T(2,128)(2,1)} %reshape.211), calls=%async_computation.5 | async-start | bytes 65536 | tf_op jit(solution)/shard_map/all_to_all | solution.py:121
  339.8 43.6 %all-to-all-start.4 = ((bf16[16,32,512]{2,0,1:T(8,128)(2,1)}), bf16[16,32,512]{2,0,1:T(8,128)(2,1)S(1)}, u32[]{:S(2)}, u32[]{:S(2)}) async-start(bf16[16,32,512]{2,0,1:T(8,128)(2,1)} %fusion.22), calls=%async_computation.4 | async-start | bytes 1048576 | tf_op jit(solution)/shard_map/all_to_all | solution.py:118
where the time goes:
time: 389 us; the launch traced here: 385 us
  other arithmetic  127 us (33%)
  waiting for transfers between devices  94.4 us (24%)
  matrix products  61.1 us (16%)
  starting transfers between devices  53.5 us (14%)
  local copies, waits for them, and re-layouts  47.5 us (12%)
    convert_element_type x2, other arithmetic, shards(): scaled.T[:, :, None].astype(jnp.bfloat16)  124 us
    dot_general x26, matrix products, contract(): return jnp.einsum(form, table, operand, precision=lax.Precision.HIGHEST)  61.1 us
    all_to_all x1, waiting for transfers between devices, shards(): lax.all_to_all(gate.T, 'ctx', split_axis=0, concat_axis=1, tiled=True)  37 us
    all_to_all x1, waiting for transfers between devices, shards(): lax.all_to_all(grad_out.T, 'ctx', split_axis=0, concat_axis=1, tiled=True)  20.2 us
    unnamed x19, local copies, waits for them, and re-layouts  18.5 us
    all_to_all x1, waiting for transfers between devices, shards(): lax.all_to_all(grads_cols, 'ctx', split_axis=1, concat_axis=0, tiled=True)  15.5 us
    all_to_all x1, starting transfers between devices, shards(): lax.all_to_all(filter_taps, 'dp', split_axis=2, concat_axis=0, tiled=True)  13 us
    all_to_all x1, starting transfers between devices, shards(): lax.all_to_all(gate.T, 'ctx', split_axis=0, concat_axis=1, tiled=True)  12.8 us
  transfers between devices with their start and end apart: 6, of which 6 were waited for; matrix products, arithmetic and copies ran while one was open for 11% of the time, Pallas kernels for 0%

commit v1 on v0

v1 whole, which is shorter than its diff:
```python
import functools

import jax
import jax.numpy as jnp
from jax import lax
from jax.experimental import pallas as pl
from jax.experimental.pallas import tpu as pltpu
from jax.sharding import PartitionSpec as P

MESH = pl.DeviceIdType.MESH
BF16 = jnp.bfloat16
F32 = jnp.float32

N_DP = 16
N_SLOT = 16
GROUP = 16
BLK = 512
T = 128
HALF = 256
PAD = 7
N_T = 128
COL = 32


def remote(src, dst, send, recv, device):
    return pltpu.make_async_remote_copy(
        src_ref=src, dst_ref=dst, send_sem=send, recv_sem=recv, device_id=device, device_id_type=MESH
    )


def loop(lower, upper, body):
    def step(i, carry):
        body(i)
        return carry

    lax.fori_loop(lower, upper, step, 0)


def kernel(
    value_hbm, gate_hbm, cot_hbm, taps_hbm, skip_hbm,
    out_ref, fg_ref,
    val, gat, cot, taps, skip,
    vloc, gloc, cot_t, tap_rows, taps_in, toep, vpad, gpad, vt, acc, lags, diag, lo, lo_in, fg, fg_in,
    in_sem, v_sem, g_sem, z_sem, tap_sem, lo_sem, fg_sem,
):
    dp = lax.axis_index("dp")
    ctx = lax.axis_index("ctx")
    side = lax.rem(ctx, 2)
    yx = ctx // 2
    col = dp * 2 + side

    def plane_peer(i):
        return lax.rem(yx + i, N_SLOT)

    def plane_device(i):
        return (dp, plane_peer(i) * 2 + side)

    def plane_source(i):
        return lax.rem(yx + N_SLOT - i, N_SLOT)

    def column_peer(r):
        return lax.rem(col + r, COL)

    def column_device(r):
        peer = column_peer(r)
        return (peer // 2, yx * 2 + lax.rem(peer, 2))

    def column_source(r):
        return lax.rem(col + COL - r, COL)

    partner = (dp, yx * 2 + 1 - side)

    barrier = pltpu.get_barrier_semaphore()
    loop(1, N_SLOT, lambda i: pl.semaphore_signal(barrier, inc=1, device_id=plane_device(i), device_id_type=MESH))
    loop(1, COL, lambda r: pl.semaphore_signal(barrier, inc=1, device_id=column_device(r), device_id_type=MESH))

    loads = [
        pltpu.make_async_copy(src, dst, in_sem.at[n])
        for n, (src, dst) in enumerate(
            ((value_hbm, val), (taps_hbm, taps), (cot_hbm, cot), (gate_hbm, gat), (skip_hbm, skip))
        )
    ]
    for load in loads:
        load.start()

    loads[0].wait()
    vloc[...] = val[...].T.reshape(N_SLOT, 2, GROUP, BLK)
    loads[1].wait()
    for c in range(8):
        tap_rows[:, c, :] = taps[:, c * T : (c + 1) * T]
    for g in range(2):
        for half in range(2):
            vpad[half, g, :HALF] = jnp.zeros((HALF, BLK), BF16)
        gpad[g, HALF:] = jnp.zeros((HALF, BLK), BF16)
        vpad[0, g, pl.ds(pl.multiple_of(HALF + yx * GROUP, GROUP), GROUP)] = vloc[yx, g]
        taps_own = taps_in.at[side, dp]
    taps_own[...] = tap_rows[dp]

    pl.semaphore_wait(barrier, N_SLOT - 1 + COL - 1)

    def v_copy(g, i, slot_at_receiver):
        return remote(
            vloc.at[plane_peer(i), g],
            vpad.at[0, g, pl.ds(pl.multiple_of(HALF + slot_at_receiver * GROUP, GROUP), GROUP)],
            v_sem.at[0, g, i], v_sem.at[1, g, i], plane_device(i),
        )

    def g_copy(g, i, slot_at_receiver):
        return remote(
            gloc.at[plane_peer(i), g],
            gpad.at[g, pl.ds(pl.multiple_of(slot_at_receiver * GROUP, GROUP), GROUP)],
            g_sem.at[0, g, i], g_sem.at[1, g, i], plane_device(i),
        )

    def z_copy(g, h, i):
        rows = pl.ds(pl.multiple_of(HALF + plane_source(i) * GROUP, GROUP), GROUP)
        cols = pl.ds(h * HALF, HALF)
        return remote(
            vpad.at[0, g, rows, cols], vpad.at[1, g, rows, cols],
            z_sem.at[0, g, h, i], z_sem.at[1, g, h, i], partner,
        )

    def tap_copy(r, half, row):
        return remote(
            tap_rows.at[column_peer(r) // 2], taps_in.at[half, row],
            tap_sem.at[0, r], tap_sem.at[1, r], column_device(r),
        )

    def lo_copy(g, i, slot_at_receiver):
        return remote(
            lo.at[g, pl.ds(pl.multiple_of(plane_peer(i) * GROUP, GROUP), GROUP)],
            lo_in.at[slot_at_receiver, g],
            lo_sem.at[0, g, i], lo_sem.at[1, g, i], plane_device(i),
        )

    def fg_copy(r, row, half):
        peer = column_peer(r)
        return remote(
            fg.at[lax.rem(peer, 2), peer // 2], fg_in.at[row, half],
            fg_sem.at[0, r], fg_sem.at[1, r], column_device(r),
        )

    loop(1, N_SLOT, lambda i: v_copy(0, i, yx).start())
    for h in range(2):
        z_copy(0, h, 0).start()
    loop(1, N_SLOT, lambda i: v_copy(1, i, yx).start())
    loop(1, COL, lambda r: tap_copy(r, side, dp).start())

    loads[2].wait()
    loads[3].wait()
    gloc[...] = (gat[...].astype(F32) * cot[...].astype(F32)).astype(BF16).T.reshape(N_SLOT, 2, GROUP, BLK)
    for g in range(2):
        loop(1, N_SLOT, lambda i, g=g: g_copy(g, i, yx).start())
        gpad[g, pl.ds(pl.multiple_of(yx * GROUP, GROUP), GROUP)] = gloc[yx, g]

    def pass_on(i):
        v_copy(0, i, plane_source(i)).wait_recv()
        z_copy(0, 0, i).start()

    loop(1, N_SLOT, pass_on)
    loop(1, N_SLOT, lambda i: z_copy(0, 1, i).start())

    cot_t[...] = cot[...].T.reshape(N_SLOT, 2, GROUP, BLK)

    rows_at = lax.broadcasted_iota(jnp.int32, (T, T), 0)
    lanes_at = lax.broadcasted_iota(jnp.int32, (T, T), 1)
    upper = lanes_at >= rows_at

    loop(1, COL, lambda r: tap_copy(r, lax.rem(column_source(r), 2), column_source(r) // 2).wait_recv())
    for g in range(2):
        toep[g, :PAD] = jnp.zeros((PAD, T, T), BF16)

        def build(d, before, g=g):
            for c in range(8):
                row = taps_in[g, d, c : c + 1, :]
                turned = pltpu.roll(jnp.broadcast_to(row, (T, T)), 0, 1, stride=1, stride_axis=0)
                toep[g, PAD + d * 8 + c] = jnp.where(upper, turned, before).astype(BF16)
                before = turned
            return before

        lax.fori_loop(0, N_DP, build, jnp.zeros((T, T), F32))

        def clear(n, g=g):
            lags[g, n] = jnp.zeros((T, T), F32)

        loop(0, N_T + PAD + 1, clear)
        acc[g] = jnp.zeros((HALF, BLK), F32)

    def lag_of(half, d):
        return 2 * d if half == 0 else 2 * d + 2 * side - 1

    def convolve(half, g, hs):
        lanes = slice(hs[0] * HALF, (hs[-1] + 1) * HALF)

        def step(d):
            k = lag_of(half, d)
            left = vpad[half, g, pl.ds(pl.multiple_of((N_SLOT - d) * GROUP, GROUP), HALF), lanes]
            us = [2 * h + e for h in hs for e in range(2)]
            tiles = {n: toep[g, 4 * k + n + PAD] for n in range(-us[-1], 4 - us[0])}
            right = jnp.concatenate(
                [jnp.concatenate([tiles[v - u] for v in range(4)], axis=1) for u in us], axis=0
            )
            acc[g] += jnp.dot(left, right, preferred_element_type=F32)

        loop(0, N_SLOT, step)

    def correlate(half, g, hs):
        lanes = slice(hs[0] * HALF, (hs[-1] + 1) * HALF)
        depth = HALF * len(hs)
        vt[:depth] = vpad[half, g, HALF:, lanes].T

        def step(d):
            k = lag_of(half, d)
            right = gpad[g, pl.ds(pl.multiple_of(d * GROUP, GROUP), HALF), :]
            product = jnp.dot(vt[:depth], right, preferred_element_type=F32)
            ws = [2 * h + e for h in hs for e in range(2)]
            for n in range(-ws[-1], 4 - ws[0]):
                terms = [
                    product[at * T : (at + 1) * T, (w + n) * T : (w + n + 1) * T]
                    for at, w in enumerate(ws)
                    if 0 <= w + n < 4
                ]
                lags[g, 4 * k + n + PAD] += functools.reduce(lambda a, b: a + b, terms)

        loop(0, N_SLOT, step)

    def finish_conv(g):
        scale = skip[pl.ds(pl.multiple_of(yx * 2 * GROUP + g * GROUP, GROUP), GROUP), :]
        scale = jnp.broadcast_to(scale[:, None, :], (GROUP, 4, T)).reshape(GROUP, BLK)

        def piece(n):
            rows = pl.ds(pl.multiple_of(n * GROUP, GROUP), GROUP)
            wide = vpad[0, g, pl.ds(pl.multiple_of(HALF + n * GROUP, GROUP), GROUP), :].astype(F32)
            lo[g, rows, :] = (acc[g, rows, :] * (1.0 / 128.0) + scale * wide).astype(BF16)

        loop(0, N_SLOT, piece)
        loop(1, N_SLOT, lambda i: lo_copy(g, i, yx).start())
        lo_in[yx, g] = lo[g, pl.ds(pl.multiple_of(yx * GROUP, GROUP), GROUP), :]

    def finish_corr(g):
        def strip(d):
            for c in range(8):
                at = PAD + d * 8 + c
                mixed = jnp.where(upper, lags[g, at], lags[g, at + 1])
                diag[d * 8 + c] = functools.reduce(
                    lambda a, b: a + b,
                    [pltpu.roll(mixed[q : q + 8], (T - q) % T, 1) for q in range(0, T, 8)],
                )

        loop(0, N_DP, strip)
        total = functools.reduce(
            lambda a, b: a + b, [pltpu.roll(diag[:, q, :], (T - q) % T, 1) for q in range(8)]
        )
        fg[g] = total.reshape(N_DP, 8, T)

        def send(r):
            @pl.when(lax.rem(column_peer(r), 2) == g)
            def _():
                fg_copy(r, dp, side).start()

        loop(1, COL, send)

    def gate_grad(g):
        loop(1, N_SLOT, lambda i: lo_copy(g, i, plane_source(i)).wait_recv())

        def piece(n):
            wide = lo_in[n, g].astype(F32) * cot_t[n, g].astype(F32)
            out_ref[pl.ds(pl.multiple_of(n * 2 * GROUP + g * GROUP, GROUP), GROUP), :] = wide.astype(BF16)

        loop(0, N_SLOT, piece)

    for g in range(2):
        loop(1, N_SLOT, lambda i, g=g: g_copy(g, i, plane_source(i)).wait_recv())
        if g == 1:
            loop(1, N_SLOT, lambda i: v_copy(1, i, plane_source(i)).wait_recv())
            for h in range(2):
                loop(0, N_SLOT, lambda i, h=h: z_copy(1, h, i).start())
        convolve(0, g, (0, 1))
        correlate(0, g, (0, 1))

    loads[4].wait()
    for g in range(2):
        for h in range(2):
            loop(0, N_SLOT, lambda i, g=g, h=h: z_copy(g, h, i).wait_recv())
            convolve(1, g, (h,))
            if h == 1:
                finish_conv(g)
            correlate(1, g, (h,))
        finish_corr(g)
        if g == 0:
            gate_grad(0)

    gate_grad(1)
    loop(1, COL, lambda r: fg_copy(r, column_source(r) // 2, lax.rem(column_source(r), 2)).wait_recv())
    fg_in[dp, side] = fg[side, dp]
    for c in range(8):
        fg_ref[:, c * T : (c + 1) * T] = (fg_in[:, 0, c, :] + fg_in[:, 1, c, :]) * (1.0 / 512.0)

    for g in range(2):

        def sent(i, g=g):
            v_copy(g, i, yx).wait_send()
            g_copy(g, i, yx).wait_send()
            lo_copy(g, i, yx).wait_send()

        loop(1, N_SLOT, sent)
        for h in range(2):
            loop(0, N_SLOT, lambda i, g=g, h=h: z_copy(g, h, i).wait_send())

    def sent_column(r):
        tap_copy(r, side, dp).wait_send()
        fg_copy(r, dp, side).wait_send()

    loop(1, COL, sent_column)


def shards(value, gate, grad_out, filter_taps, skip):
    taps = filter_taps[:, 0, :].T
    skip_wide = jnp.broadcast_to(skip[:, None], (BLK, T))
    any_spec = pl.BlockSpec(memory_space=pl.ANY)
    vmem_spec = pl.BlockSpec(memory_space=pltpu.VMEM)
    grad_t, fg = pl.pallas_call(
        kernel,
        out_shape=(
            jax.ShapeDtypeStruct((BLK, BLK), BF16),
            jax.ShapeDtypeStruct((N_DP, 1024), F32),
        ),
        in_specs=[any_spec] * 5,
        out_specs=(vmem_spec, vmem_spec),
        scratch_shapes=[
            pltpu.VMEM((BLK, BLK), BF16),
            pltpu.VMEM((BLK, BLK), BF16),
            pltpu.VMEM((BLK, BLK), BF16),
            pltpu.VMEM((N_DP, 1024), F32),
            pltpu.VMEM((BLK, T), F32),
            pltpu.VMEM((N_SLOT, 2, GROUP, BLK), BF16),
            pltpu.VMEM((N_SLOT, 2, GROUP, BLK), BF16),
            pltpu.VMEM((N_SLOT, 2, GROUP, BLK), BF16),
            pltpu.VMEM((N_DP, 8, T), F32),
            pltpu.VMEM((2, N_DP, 8, T), F32),
            pltpu.VMEM((2, N_T + PAD, T, T), BF16),
            pltpu.VMEM((2, 2, BLK, BLK), BF16),
            pltpu.VMEM((2, BLK, BLK), BF16),
            pltpu.VMEM((BLK, HALF), BF16),
            pltpu.VMEM((2, HALF, BLK), F32),
            pltpu.VMEM((2, N_T + PAD + 1, T, T), F32),
            pltpu.VMEM((N_T, 8, T), F32),
            pltpu.VMEM((2, HALF, BLK), BF16),
            pltpu.VMEM((N_SLOT, 2, GROUP, BLK), BF16),
            pltpu.VMEM((2, N_DP, 8, T), F32),
            pltpu.VMEM((N_DP, 2, 8, T), F32),
            pltpu.SemaphoreType.DMA((5,)),
            pltpu.SemaphoreType.DMA((2, 2, N_SLOT)),
            pltpu.SemaphoreType.DMA((2, 2, N_SLOT)),
            pltpu.SemaphoreType.DMA((2, 2, 2, N_SLOT)),
            pltpu.SemaphoreType.DMA((2, COL)),
            pltpu.SemaphoreType.DMA((2, 2, N_SLOT)),
            pltpu.SemaphoreType.DMA((2, COL)),
        ],
        compiler_params=pltpu.CompilerParams(
            collective_id=0, has_side_effects=True, vmem_limit_bytes=56 * 2**20
        ),
        cost_estimate=pl.CostEstimate(flops=2 * 2**33, bytes_accessed=4 * 2**20, transcendentals=0),
        name="hyena",
    )(value, gate, grad_out, taps, skip_wide)
    return grad_t.T, fg.T[:, None, :]


def solution(mesh):
    in_specs = (P("ctx", "dp"), P("ctx", "dp"), P("ctx", "dp"), P("dp", "ctx", None), P("dp"))
    out_specs = (P("ctx", "dp"), P("dp", "ctx", None))
    return jax.shard_map(shards, mesh=mesh, in_specs=in_specs, out_specs=out_specs, check_vma=False)
```

time: 389 us -> 125 us (0.32)
  the two profiles are of different devices: /device:TPU:33 before, /device:TPU:417 now
where the time goes in v1:
time: 125 us
  Pallas kernels  120 us (96%)
  local copies, waits for them, and re-layouts  4.23 us (3%)
    pallas_call x1, Pallas kernels, shards(): pl.pallas_call(kernel, out_shape=(jax.ShapeDtypeStruct((BLK, BLK), BF16),...  120 us
    unnamed x4, local copies, waits for them, and re-layouts  2.71 us

profile of v1, /device:TPU:417, one launch (start us, length us, event | category | flops | bytes accessed | tf_op | source)
XLA Modules:
  0.0 124.6 jit_solution(14287428359337963002)
XLA Ops:
  0.6 1.5 %broadcast_in_dim.4.skip_hbm = f32[512,128]{1,0:T(8,128)} broadcast(f32[512]{0:T(512)} %param.9), dimensions={0} | broadcast | bytes 264192 | tf_op jit(solution)/shard_map/broadcast_in_dim | solution.py:319
  2.1 119.8 %hyena.1 = (bf16[512,512]{1,0:T(8,128)(2,1)}, f32[16,1024]{1,0:T(8,128)}) custom-call(bf16[512,512]{1,0:T(8,128)(2,1)} %value_hbm.1, bf16[512,512]{1,0:T(8,128)(2,1)} %gate_hbm.1, bf16[512,512]{1,0:T(8,128)(2,1)} %cot_hbm.1, f32[16,1024]{1,0:T(8,128)} %bitcast.9, f32[512,128]{1,0:T(8,128)} %broadcast_in_dim.4.skip_hbm), custom_call_target="tpu_custom_call" | custom-call | flops 17179869184 | bytes 4194304 | tf_op jit(solution)/shard_map/hyena/pallas_call | solution.py:322
  121.9 0.0 copy-start
  121.9 2.1 %copy.7 = bf16[512,512]{1,0:T(8,128)(2,1)} copy(bf16[512,512]{0,1:T(8,128)(2,1)} %bitcast.7) | data formatting | bytes 1048576
  124.0 0.0 copy-done
  124.0 0.6 copy.9
Async XLA Ops:
  121.9 2.1 %copy-start = (f32[16,1024]{1,0:T(8,128)S(1)}, f32[16,1024]{1,0:T(8,128)}, u32[]{:S(2)}) copy-start(f32[16,1024]{1,0:T(8,128)} %get-tuple-element.5) | copy-start | bytes 196612

commit v2 on v1

v2 whole, which is shorter than its diff:
```python
import functools

import jax
import jax.numpy as jnp
from jax import lax
from jax.experimental import pallas as pl
from jax.experimental.pallas import tpu as pltpu
from jax.sharding import PartitionSpec as P

MESH = pl.DeviceIdType.MESH
BF16 = jnp.bfloat16
F32 = jnp.float32

N_DP = 16
N_SLOT = 16
GROUP = 16
BLK = 512
T = 128
HALF = 256
PAD = 7
N_T = 128
PILE = 16


def remote(src, dst, send, recv, device):
    return pltpu.make_async_remote_copy(
        src_ref=src, dst_ref=dst, send_sem=send, recv_sem=recv, device_id=device, device_id_type=MESH
    )


def loop(lower, upper, body):
    def step(i, carry):
        body(i)
        return carry

    lax.fori_loop(lower, upper, step, 0)


def kernel(
    value_hbm, gate_hbm, cot_hbm, taps_hbm, skip_hbm,
    out_ref, fg_ref,
    val, gat, cot, taps, skip, skip_rows,
    vloc, gloc, tap_own, tap_sib, tap_mix, taps_in, toep, relay, vals, gpad, acc, lags, diag, lo, lo_in,
    fg, fg_in, fg_own, fg_sib, fg_rows,
    in_sem, v_sem, g_sem, r_sem, z_sem, tap_sem, lo_sem, fg_sem, sib_sem,
):
    dp = lax.axis_index("dp")
    ctx = lax.axis_index("ctx")
    core = lax.rem(dp, 2)
    side = lax.rem(ctx, 2)
    yx = ctx // 2
    z = side * 8 + dp // 2
    z_lo = dp // 2
    pile = z_lo * 2 + side
    sibling = (dp + 1 - 2 * core, ctx)

    def device(z_at, yx_at):
        z_at = lax.rem(z_at + 16, 16)
        return (lax.rem(z_at, 8) * 2 + core, yx_at * 2 + z_at // 8)

    def plane_peer(i):
        return lax.rem(yx + i, N_SLOT)

    def plane_device(i):
        return (dp, plane_peer(i) * 2 + side)

    def plane_source(i):
        return lax.rem(yx + N_SLOT - i, N_SLOT)

    def pile_peer(r):
        return lax.rem(pile + r, PILE)

    def pile_device(r):
        peer = pile_peer(r)
        return (peer // 2 * 2 + core, yx * 2 + lax.rem(peer, 2))

    def pile_source(r):
        return lax.rem(pile + PILE - r, PILE)

    def way(i):
        return 1 - 2 * lax.rem(i, 2)

    def rows_at(slot):
        return pl.ds(pl.multiple_of(slot * GROUP, GROUP), GROUP)

    barrier = pltpu.get_barrier_semaphore()

    def greet(target):
        pl.semaphore_signal(barrier, inc=1, device_id=target, device_id_type=MESH)

    loop(1, PILE, lambda r: greet(pile_device(r)))
    greet(sibling)
    loop(1, N_SLOT, lambda i: greet(device(z - way(i), plane_source(i))))
    loop(1, N_SLOT, lambda i: greet(plane_device(i)))

    loads = [
        pltpu.make_async_copy(src, dst, in_sem.at[n])
        for n, (src, dst) in enumerate(
            ((value_hbm, val), (taps_hbm, taps), (cot_hbm, cot), (gate_hbm, gat), (skip_hbm, skip))
        )
    ]
    for load in loads:
        load.start()

    loads[0].wait()
    vloc[...] = val[...].T.reshape(N_SLOT, 2, GROUP, BLK)
    loads[1].wait()
    for b in range(N_DP):
        for c in range(8):
            tap_own[b % 2, b // 2, c : c + 1, :] = taps[b : b + 1, c * T : (c + 1) * T]
    for g in range(2):
        gpad[g, HALF:] = jnp.zeros((HALF, BLK), BF16)
        vals[0, g, rows_at(yx)] = vloc[yx, g]

    pl.semaphore_wait(barrier, PILE + 2 * (N_SLOT - 1))

    def r_copy(g, i, slot_at_receiver):
        return remote(
            vloc.at[plane_peer(i), g], relay.at[g, rows_at(slot_at_receiver)],
            r_sem.at[0, g, i], r_sem.at[1, g, i], device(z + way(i), plane_peer(i)),
        )

    def z_copy(g, h, i):
        lanes = pl.ds(pl.multiple_of(h * HALF, HALF), HALF)
        slot = plane_source(i)
        return remote(
            relay.at[g, rows_at(slot), lanes], vals.at[1, g, rows_at(slot), lanes],
            z_sem.at[0, g, h, i], z_sem.at[1, g, h, i], device(z + 7 * way(i), yx),
        )

    def v_copy(g, i, slot_at_receiver):
        return remote(
            vloc.at[plane_peer(i), g], vals.at[0, g, rows_at(slot_at_receiver)],
            v_sem.at[0, g, i], v_sem.at[1, g, i], plane_device(i),
        )

    def g_copy(g, i, slot_at_receiver):
        return remote(
            gloc.at[plane_peer(i), g], gpad.at[g, rows_at(slot_at_receiver)],
            g_sem.at[0, g, i], g_sem.at[1, g, i], plane_device(i),
        )

    tap_trade = remote(tap_own.at[1 - core], tap_sib, sib_sem.at[0, 0], sib_sem.at[1, 0], sibling)
    fg_trade = remote(fg_own.at[1 - core], fg_sib, sib_sem.at[0, 1], sib_sem.at[1, 1], sibling)

    def tap_copy(r, half, row):
        return remote(
            tap_mix.at[pile_peer(r) // 2], taps_in.at[half, row],
            tap_sem.at[0, r], tap_sem.at[1, r], pile_device(r),
        )

    def lo_copy(g, i, slot_at_receiver):
        return remote(
            lo.at[g, rows_at(plane_peer(i))], lo_in.at[slot_at_receiver, g],
            lo_sem.at[0, g, i], lo_sem.at[1, g, i], plane_device(i),
        )

    def fg_copy(r, row, half):
        peer = pile_peer(r)
        return remote(
            fg.at[lax.rem(peer, 2), peer // 2], fg_in.at[row, half],
            fg_sem.at[0, r], fg_sem.at[1, r], pile_device(r),
        )

    tap_trade.start()
    for g in range(2):
        loop(0, N_SLOT, lambda i, g=g: r_copy(g, i, yx).start())
    loop(1, N_SLOT, lambda i: v_copy(0, i, yx).start())
    tap_trade.wait_recv()
    mine, other = tap_own[core], tap_sib[...]
    tap_mix[...] = jnp.concatenate(
        [jnp.where(core == 0, mine, other), jnp.where(core == 0, other, mine)], axis=1
    ).astype(BF16)
    loop(1, PILE, lambda r: tap_copy(r, side, z_lo).start())
    taps_in[side, z_lo] = tap_mix[z_lo]
    loop(1, N_SLOT, lambda i: v_copy(1, i, yx).start())

    loads[2].wait()
    loads[3].wait()
    gloc[...] = (gat[...].astype(F32) * cot[...].astype(F32)).astype(BF16).T.reshape(N_SLOT, 2, GROUP, BLK)
    for g in range(2):
        loop(1, N_SLOT, lambda i, g=g: g_copy(g, i, yx).start())
        gpad[g, rows_at(yx)] = gloc[yx, g]

    def pass_on(i):
        r_copy(0, i, plane_source(i)).wait_recv()
        z_copy(0, 0, i).start()

    loop(0, N_SLOT, pass_on)
    loop(0, N_SLOT, lambda i: z_copy(0, 1, i).start())

    loads[4].wait()
    skip_rows[...] = jnp.broadcast_to(skip[...], (T, BLK)).T

    q_at = lax.broadcasted_iota(jnp.int32, (T, T), 0)
    p_at = lax.broadcasted_iota(jnp.int32, (T, T), 1)
    upper = p_at >= q_at

    for g in range(2):
        toep[g, :PAD] = jnp.zeros((PAD, T, T), BF16)
        for n in [0, 1, 2] + list(range(3, N_T + PAD, 8)) + list(range(N_T + 4, N_T + PAD + 1)):
            lags[g, n] = jnp.zeros((T, T), F32)

    loop(1, PILE, lambda r: tap_copy(r, lax.rem(pile_source(r), 2), pile_source(r) // 2).wait_recv())
    for g in range(2):

        def build(d, before, g=g):
            rows = taps_in[g, d].astype(F32)
            for c in range(16):
                turned = pltpu.roll(jnp.broadcast_to(rows[c : c + 1], (T, T)), 0, 1, stride=1, stride_axis=0)
                toep[g, PAD + d * 16 + c] = jnp.where(upper, turned, before).astype(BF16)
                before = turned
            return before

        lax.fori_loop(0, 8, build, jnp.zeros((T, T), F32))

    def convolve(half, g, h, width):
        lanes = pl.ds(pl.multiple_of(h * HALF, HALF), width * HALF)
        for d in range(N_SLOT):
            base = 8 * d + PAD if half == 0 else 8 * d + 8 * side - 4 - 2 * h + PAD
            left = vals[half, g, : HALF - d * GROUP, lanes]
            tiles = {n: toep[g, base + n] for n in range(1 - 2 * width, 4)}
            right = jnp.concatenate(
                [jnp.concatenate([tiles[v - u] for v in range(4)], axis=1) for u in range(2 * width)], axis=0
            )
            product = jnp.dot(left, right, preferred_element_type=F32)
            if half == 0 and d == 0:
                acc[g] = product
            else:
                acc[g, d * GROUP :] += product

    def correlate(half, g, h, width):
        lanes = pl.ds(pl.multiple_of(h * HALF, HALF), width * HALF)
        left = vals[half, g, :, lanes].T
        for d in range(N_SLOT):
            base = 8 * d + PAD if half == 0 else 8 * d + 8 * side - 4 - 2 * h + PAD
            right = gpad[g, d * GROUP : d * GROUP + HALF, :]
            product = jnp.dot(left, right, preferred_element_type=F32)
            for n in range(1 - 2 * width, 4):
                part = functools.reduce(
                    lambda a, b: a + b,
                    [
                        product[w * T : (w + 1) * T, (w + n) * T : (w + n + 1) * T]
                        for w in range(2 * width)
                        if 0 <= w + n < 4
                    ],
                )
                if half == 0:
                    lags[g, base + n] = part
                else:
                    lags[g, base + n] += part

    def finish_conv(g):
        scale = skip_rows[pl.ds(pl.multiple_of((yx * 2 + g) * GROUP, GROUP), GROUP), :]
        scale = jnp.concatenate([scale] * 4, axis=1)
        for n in range(N_SLOT):
            wide = vals[0, g, n * GROUP : (n + 1) * GROUP, :].astype(F32)
            rows = slice(n * GROUP, (n + 1) * GROUP)
            lo[g, rows, :] = (acc[g, rows, :] * (1.0 / 128.0) + scale * wide).astype(BF16)
        loop(1, N_SLOT, lambda i: lo_copy(g, i, yx).start())
        lo_in[yx, g] = lo[g, rows_at(yx), :]

    def finish_corr(g):
        def strip(d):
            for c in range(8):
                at = PAD + d * 8 + c
                mixed = jnp.where(upper, lags[g, at], lags[g, at + 1])
                diag[d * 8 + c] = functools.reduce(
                    lambda a, b: a + b,
                    [pltpu.roll(mixed[q : q + 8], (T - q) % T, 1) for q in range(0, T, 8)],
                )

        loop(0, N_DP, strip)
        total = functools.reduce(
            lambda a, b: a + b, [pltpu.roll(diag[:, q, :], (T - q) % T, 1) for q in range(8)]
        )
        fg[g] = total.reshape(8, 16, T).astype(BF16)

        def send(r):
            @pl.when(lax.rem(pile_peer(r), 2) == g)
            def _():
                fg_copy(r, z_lo, side).start()

        loop(1, PILE, send)

    loop(0, N_SLOT, lambda i: r_copy(1, i, plane_source(i)).wait_recv())
    for g in range(2):

        def arrived(i, g=g):
            v_copy(g, i, plane_source(i)).wait_recv()
            g_copy(g, i, plane_source(i)).wait_recv()

        loop(1, N_SLOT, arrived)

    def own(g):
        convolve(0, g, 0, 2)
        correlate(0, g, 0, 2)

    loop(0, 2, own)

    def phase(n):
        g = n // 2
        h = lax.rem(n, 2)
        loop(0, N_SLOT, lambda i: z_copy(g, h, i).wait_recv())

        @pl.when(g == 0)
        def _():
            loop(0, N_SLOT, lambda i: z_copy(1, h, i).start())

        convolve(1, g, h, 1)

        @pl.when(h == 1)
        def _():
            finish_conv(g)

        correlate(1, g, h, 1)

        @pl.when(h == 1)
        def _():
            finish_corr(g)

    loop(0, 4, phase)

    for g in range(2):
        loop(1, N_SLOT, lambda i, g=g: lo_copy(g, i, plane_source(i)).wait_recv())
    long_out = lo_in[...].reshape(BLK, BLK).T
    out_ref[...] = (long_out.astype(F32) * cot[...].astype(F32)).astype(BF16)

    loop(1, PILE, lambda r: fg_copy(r, pile_source(r) // 2, lax.rem(pile_source(r), 2)).wait_recv())
    fg_in[z_lo, side] = fg[side, z_lo]
    both = (fg_in[:, 0].astype(F32) + fg_in[:, 1].astype(F32)) * (1.0 / 512.0)
    fg_own[0] = both[:, :8]
    fg_own[1] = both[:, 8:]
    fg_trade.start()
    fg_trade.wait_recv()
    mine, other = fg_own[core], fg_sib[...]
    fg_rows[:, 0] = jnp.where(core == 0, mine, other)
    fg_rows[:, 1] = jnp.where(core == 0, other, mine)
    for b in range(N_DP):
        for c in range(8):
            fg_ref[b : b + 1, c * T : (c + 1) * T] = fg_rows[b // 2, b % 2, c : c + 1, :]

    tap_trade.wait_send()
    fg_trade.wait_send()
    for g in range(2):

        def sent(i, g=g):
            v_copy(g, i, yx).wait_send()
            g_copy(g, i, yx).wait_send()
            lo_copy(g, i, yx).wait_send()

        loop(1, N_SLOT, sent)

        def sent_over(i, g=g):
            r_copy(g, i, yx).wait_send()
            for h in range(2):
                z_copy(g, h, i).wait_send()

        loop(0, N_SLOT, sent_over)

    def sent_column(r):
        tap_copy(r, side, z_lo).wait_send()
        fg_copy(r, z_lo, side).wait_send()

    loop(1, PILE, sent_column)


def shards(value, gate, grad_out, filter_taps, skip):
    taps = filter_taps[:, 0, :].T
    any_spec = pl.BlockSpec(memory_space=pl.ANY)
    vmem_spec = pl.BlockSpec(memory_space=pltpu.VMEM)
    grad, fg = pl.pallas_call(
        kernel,
        out_shape=(
            jax.ShapeDtypeStruct((BLK, BLK), BF16),
            jax.ShapeDtypeStruct((N_DP, 1024), F32),
        ),
        in_specs=[any_spec] * 5,
        out_specs=(vmem_spec, vmem_spec),
        scratch_shapes=[
            pltpu.VMEM((BLK, BLK), BF16),
            pltpu.VMEM((BLK, BLK), BF16),
            pltpu.VMEM((BLK, BLK), BF16),
            pltpu.VMEM((N_DP, 1024), F32),
            pltpu.VMEM((1, BLK), F32),
            pltpu.VMEM((BLK, T), F32),
            pltpu.VMEM((N_SLOT, 2, GROUP, BLK), BF16),
            pltpu.VMEM((N_SLOT, 2, GROUP, BLK), BF16),
            pltpu.VMEM((2, 8, 8, T), F32),
            pltpu.VMEM((8, 8, T), F32),
            pltpu.VMEM((8, 16, T), BF16),
            pltpu.VMEM((2, 8, 16, T), BF16),
            pltpu.VMEM((2, N_T + PAD, T, T), BF16),
            pltpu.VMEM((2, HALF, BLK), BF16),
            pltpu.VMEM((2, 2, HALF, BLK), BF16),
            pltpu.VMEM((2, BLK, BLK), BF16),
            pltpu.VMEM((2, HALF, BLK), F32),
            pltpu.VMEM((2, N_T + PAD + 1, T, T), F32),
            pltpu.VMEM((N_T, 8, T), F32),
            pltpu.VMEM((2, HALF, BLK), BF16),
            pltpu.VMEM((N_SLOT, 2, GROUP, BLK), BF16),
            pltpu.VMEM((2, 8, 16, T), BF16),
            pltpu.VMEM((8, 2, 16, T), BF16),
            pltpu.VMEM((2, 8, 8, T), F32),
            pltpu.VMEM((8, 8, T), F32),
            pltpu.VMEM((8, 2, 8, T), F32),
            pltpu.SemaphoreType.DMA((5,)),
            pltpu.SemaphoreType.DMA((2, 2, N_SLOT)),
            pltpu.SemaphoreType.DMA((2, 2, N_SLOT)),
            pltpu.SemaphoreType.DMA((2, 2, N_SLOT)),
            pltpu.SemaphoreType.DMA((2, 2, 2, N_SLOT)),
            pltpu.SemaphoreType.DMA((2, PILE)),
            pltpu.SemaphoreType.DMA((2, 2, N_SLOT)),
            pltpu.SemaphoreType.DMA((2, PILE)),
            pltpu.SemaphoreType.DMA((2, 2)),
        ],
        compiler_params=pltpu.CompilerParams(
            collective_id=0, has_side_effects=True, vmem_limit_bytes=56 * 2**20
        ),
        cost_estimate=pl.CostEstimate(flops=2 * 2**33, bytes_accessed=4 * 2**20, transcendentals=0),
        name="hyena",
    )(value, gate, grad_out, taps, skip[None, :])
    return grad, fg.T[:, None, :]


def solution(mesh):
    in_specs = (P("ctx", "dp"), P("ctx", "dp"), P("ctx", "dp"), P("dp", "ctx", None), P("dp"))
    out_specs = (P("ctx", "dp"), P("dp", "ctx", None))
    return jax.shard_map(shards, mesh=mesh, in_specs=in_specs, out_specs=out_specs, check_vma=False)
```

time: 125 us -> 92.9 us (0.74)
  Pallas kernels: 120 us -> 89.5 us
  local copies, waits for them, and re-layouts: 4.23 us -> 2.53 us
    pallas_call x1, Pallas kernels: 120 us -> 89.5 us  [shards(): pl.pallas_call(kernel, out_shape=(jax.ShapeDtypeStruct((BLK, BLK), BF16),...]
    broadcast_in_dim x1 -> x0, local copies, waits for them, and re-layouts: 1.52 us -> none  [shards(): skip_wide = jnp.broadcast_to(skip[:, None], (BLK, T))]
where the time goes in v2:
time: 92.9 us; the launch traced here: 92.7 us
  Pallas kernels  89.5 us (96%)
  local copies, waits for them, and re-layouts  2.53 us (3%)
    pallas_call x1, Pallas kernels, shards(): pl.pallas_call(kernel, out_shape=(jax.ShapeDtypeStruct((BLK, BLK), BF16),...  89.5 us
    unnamed x4, local copies, waits for them, and re-layouts  2.53 us

profile of v2, /device:TPU:417, one launch (start us, length us, event | category | flops | bytes accessed | tf_op | source)
XLA Modules:
  0.0 92.7 jit_solution(13869962586075519449)
XLA Ops:
  0.6 89.5 %hyena.1 = (bf16[512,512]{1,0:T(8,128)(2,1)}, f32[16,1024]{1,0:T(8,128)}) custom-call(bf16[512,512]{1,0:T(8,128)(2,1)} %value_hbm.1, bf16[512,512]{1,0:T(8,128)(2,1)} %gate_hbm.1, bf16[512,512]{1,0:T(8,128)(2,1)} %cot_hbm.1, f32[16,1024]{1,0:T(8,128)} %bitcast.8, f32[1,512]{1,0:T(1,128)} %bitcast.9), custom_call_target="tpu_custom_call" | custom-call | flops 17179869184 | bytes 4194304 | tf_op jit(solution)/shard_map/hyena/pallas_call | solution.py:372
  90.2 0.0 copy-start
  90.2 1.9 %copy.9 = bf16[512,512]{1,0:T(8,128)(2,1)} copy(bf16[512,512]{1,0:T(8,128)(2,1)} %get-tuple-element.8) | data formatting | bytes 1048576
  92.1 0.0 copy-done
  92.1 0.6 copy.10
Async XLA Ops:
  90.2 1.9 %copy-start = (f32[16,1024]{1,0:T(8,128)S(1)}, f32[16,1024]{1,0:T(8,128)}, u32[]{:S(2)}) copy-start(f32[16,1024]{1,0:T(8,128)} %get-tuple-element.5) | copy-start | bytes 196612

commit v3 on v2

--- a/solution.py
+++ b/solution.py
@@ -28,11 +28,15 @@
     )
 
 
-def loop(lower, upper, body):
+def loop(lower, upper, body, unroll=True):
     def step(i, carry):
         body(i)
         return carry
 
+    if upper - lower in (15, 16) and unroll:
+        for i in range(lower, upper):
+            body(i)
+        return
     lax.fori_loop(lower, upper, step, 0)
 
 
@@ -77,8 +81,8 @@
     def pile_source(r):
         return lax.rem(pile + PILE - r, PILE)
 
-    def way(i):
-        return 1 - 2 * lax.rem(i, 2)
+    def way(one, two):
+        return 1 - 2 * lax.rem(one // 8 + two // 8, 2)
 
     def rows_at(slot):
         return pl.ds(pl.multiple_of(slot * GROUP, GROUP), GROUP)
@@ -90,7 +94,7 @@
 
     loop(1, PILE, lambda r: greet(pile_device(r)))
     greet(sibling)
-    loop(1, N_SLOT, lambda i: greet(device(z - way(i), plane_source(i))))
+    loop(1, N_SLOT, lambda i: greet(device(z - way(plane_source(i), yx), plane_source(i))))
     loop(1, N_SLOT, lambda i: greet(plane_device(i)))
 
     loads = [
@@ -108,36 +112,36 @@
     for b in range(N_DP):
         for c in range(8):
             tap_own[b % 2, b // 2, c : c + 1, :] = taps[b : b + 1, c * T : (c + 1) * T]
-    for g in range(2):
-        gpad[g, HALF:] = jnp.zeros((HALF, BLK), BF16)
-        vals[0, g, rows_at(yx)] = vloc[yx, g]
+    loads[2].wait()
+    loads[3].wait()
+    gloc[...] = (gat[...].astype(F32) * cot[...].astype(F32)).astype(BF16).T.reshape(N_SLOT, 2, GROUP, BLK)
 
     pl.semaphore_wait(barrier, PILE + 2 * (N_SLOT - 1))
 
-    def r_copy(g, i, slot_at_receiver):
-        return remote(
-            vloc.at[plane_peer(i), g], relay.at[g, rows_at(slot_at_receiver)],
-            r_sem.at[0, g, i], r_sem.at[1, g, i], device(z + way(i), plane_peer(i)),
-        )
-
-    def z_copy(g, h, i):
+    def r_copy(i, slot_at_receiver):
+        return remote(
+            vloc.at[plane_peer(i)], relay.at[:, rows_at(slot_at_receiver)],
+            r_sem.at[0, i], r_sem.at[1, i], device(z + way(yx, plane_peer(i)), plane_peer(i)),
+        )
+
+    def z_copy(g, h, half):
+        rows = pl.ds(half * (HALF // 2), HALF // 2)
         lanes = pl.ds(pl.multiple_of(h * HALF, HALF), HALF)
-        slot = plane_source(i)
-        return remote(
-            relay.at[g, rows_at(slot), lanes], vals.at[1, g, rows_at(slot), lanes],
-            z_sem.at[0, g, h, i], z_sem.at[1, g, h, i], device(z + 7 * way(i), yx),
-        )
-
-    def v_copy(g, i, slot_at_receiver):
-        return remote(
-            vloc.at[plane_peer(i), g], vals.at[0, g, rows_at(slot_at_receiver)],
-            v_sem.at[0, g, i], v_sem.at[1, g, i], plane_device(i),
-        )
-
-    def g_copy(g, i, slot_at_receiver):
-        return remote(
-            gloc.at[plane_peer(i), g], gpad.at[g, rows_at(slot_at_receiver)],
-            g_sem.at[0, g, i], g_sem.at[1, g, i], plane_device(i),
+        return remote(
+            relay.at[g, rows, lanes], vals.at[1, g, rows, lanes],
+            z_sem.at[0, g, h, half], z_sem.at[1, g, h, half], device(z + 7 * way(8 * half, yx), yx),
+        )
+
+    def v_copy(i, slot_at_receiver):
+        return remote(
+            vloc.at[plane_peer(i)], vals.at[0, :, rows_at(slot_at_receiver)],
+            v_sem.at[0, i], v_sem.at[1, i], plane_device(i),
+        )
+
+    def g_copy(i, slot_at_receiver):
+        return remote(
+            gloc.at[plane_peer(i)], gpad.at[:, rows_at(slot_at_receiver)],
+            g_sem.at[0, i], g_sem.at[1, i], plane_device(i),
         )
 
     tap_trade = remote(tap_own.at[1 - core], tap_sib, sib_sem.at[0, 0], sib_sem.at[1, 0], sibling)
@@ -162,32 +166,29 @@
             fg_sem.at[0, r], fg_sem.at[1, r], pile_device(r),
         )
 
+    loop(0, N_SLOT, lambda i: r_copy(i, yx).start())
     tap_trade.start()
-    for g in range(2):
-        loop(0, N_SLOT, lambda i, g=g: r_copy(g, i, yx).start())
-    loop(1, N_SLOT, lambda i: v_copy(0, i, yx).start())
+    loop(1, N_SLOT, lambda i: v_copy(i, yx).start())
     tap_trade.wait_recv()
     mine, other = tap_own[core], tap_sib[...]
     tap_mix[...] = jnp.concatenate(
         [jnp.where(core == 0, mine, other), jnp.where(core == 0, other, mine)], axis=1
     ).astype(BF16)
     loop(1, PILE, lambda r: tap_copy(r, side, z_lo).start())
+    loop(1, N_SLOT, lambda i: g_copy(i, yx).start())
+
+    for half in range(2):
+        for n in range(8 * half, 8 * half + 8):
+            r_copy(lax.rem(yx + N_SLOT - n, N_SLOT), n).wait_recv()
+        z_copy(0, 0, half).start()
+    for half in range(2):
+        z_copy(0, 1, half).start()
+
     taps_in[side, z_lo] = tap_mix[z_lo]
-    loop(1, N_SLOT, lambda i: v_copy(1, i, yx).start())
-
-    loads[2].wait()
-    loads[3].wait()
-    gloc[...] = (gat[...].astype(F32) * cot[...].astype(F32)).astype(BF16).T.reshape(N_SLOT, 2, GROUP, BLK)
-    for g in range(2):
-        loop(1, N_SLOT, lambda i, g=g: g_copy(g, i, yx).start())
+    for g in range(2):
         gpad[g, rows_at(yx)] = gloc[yx, g]
-
-    def pass_on(i):
-        r_copy(0, i, plane_source(i)).wait_recv()
-        z_copy(0, 0, i).start()
-
-    loop(0, N_SLOT, pass_on)
-    loop(0, N_SLOT, lambda i: z_copy(0, 1, i).start())
+        gpad[g, HALF:] = jnp.zeros((HALF, BLK), BF16)
+        vals[0, g, rows_at(yx)] = vloc[yx, g]
 
     loads[4].wait()
     skip_rows[...] = jnp.broadcast_to(skip[...], (T, BLK)).T
@@ -264,15 +265,15 @@
         def strip(d):
             for c in range(8):
                 at = PAD + d * 8 + c
-                mixed = jnp.where(upper, lags[g, at], lags[g, at + 1])
+                mixed = jnp.where(upper, lags[g, at], lags[g, at + 1]).astype(BF16)
                 diag[d * 8 + c] = functools.reduce(
                     lambda a, b: a + b,
-                    [pltpu.roll(mixed[q : q + 8], (T - q) % T, 1) for q in range(0, T, 8)],
+                    [pltpu.roll(mixed[q : q + 16], (T - q) % T, 1).astype(F32) for q in range(0, T, 16)],
                 )
 
-        loop(0, N_DP, strip)
+        loop(0, N_DP, strip, False)
         total = functools.reduce(
-            lambda a, b: a + b, [pltpu.roll(diag[:, q, :], (T - q) % T, 1) for q in range(8)]
+            lambda a, b: a + b, [pltpu.roll(diag[:, q, :], (T - q) % T, 1) for q in range(16)]
         )
         fg[g] = total.reshape(8, 16, T).astype(BF16)
 
@@ -283,14 +284,11 @@
 
         loop(1, PILE, send)
 
-    loop(0, N_SLOT, lambda i: r_copy(1, i, plane_source(i)).wait_recv())
-    for g in range(2):
-
-        def arrived(i, g=g):
-            v_copy(g, i, plane_source(i)).wait_recv()
-            g_copy(g, i, plane_source(i)).wait_recv()
-
-        loop(1, N_SLOT, arrived)
+    def arrived(i):
+        v_copy(i, plane_source(i)).wait_recv()
+        g_copy(i, plane_source(i)).wait_recv()
+
+    loop(1, N_SLOT, arrived)
 
     def own(g):
         convolve(0, g, 0, 2)
@@ -298,14 +296,43 @@
 
     loop(0, 2, own)
 
+    def sent():
+        def plane(i):
+            v_copy(i, yx).wait_send()
+            g_copy(i, yx).wait_send()
+
+        loop(1, N_SLOT, plane)
+
+        loop(0, N_SLOT, lambda i: r_copy(i, yx).wait_send())
+        loop(1, PILE, lambda r: tap_copy(r, side, z_lo).wait_send())
+        tap_trade.wait_send()
+
+    def close_filter_grad():
+        loop(1, PILE, lambda r: fg_copy(r, pile_source(r) // 2, lax.rem(pile_source(r), 2)).wait_recv())
+        fg_in[z_lo, side] = fg[side, z_lo]
+        both = (fg_in[:, 0].astype(F32) + fg_in[:, 1].astype(F32)) * (1.0 / 512.0)
+        fg_own[0] = both[:, :8]
+        fg_own[1] = both[:, 8:]
+        fg_trade.start()
+        fg_trade.wait_recv()
+        mine, other = fg_own[core], fg_sib[...]
+        fg_rows[:, 0] = jnp.where(core == 0, mine, other)
+        fg_rows[:, 1] = jnp.where(core == 0, other, mine)
+        for b in range(N_DP):
+            for c in range(8):
+                fg_ref[b : b + 1, c * T : (c + 1) * T] = fg_rows[b // 2, b % 2, c : c + 1, :]
+
     def phase(n):
         g = n // 2
         h = lax.rem(n, 2)
-        loop(0, N_SLOT, lambda i: z_copy(g, h, i).wait_recv())
-
-        @pl.when(g == 0)
+        pl.when(n == 3)(sent)
+        for half in range(2):
+            z_copy(g, h, half).wait_recv()
+
+        @pl.when(n == 0)
         def _():
-            loop(0, N_SLOT, lambda i: z_copy(1, h, i).start())
+            for half in range(2):
+                z_copy(1, 0, half).start()
 
         convolve(1, g, h, 1)
 
@@ -319,57 +346,34 @@
         def _():
             finish_corr(g)
 
+        @pl.when(n == 1)
+        def _():
+            for half in range(2):
+                z_copy(1, 1, half).start()
+
     loop(0, 4, phase)
+    pl.when(side == 0)(close_filter_grad)
 
     for g in range(2):
         loop(1, N_SLOT, lambda i, g=g: lo_copy(g, i, plane_source(i)).wait_recv())
-    long_out = lo_in[...].reshape(BLK, BLK).T
-    out_ref[...] = (long_out.astype(F32) * cot[...].astype(F32)).astype(BF16)
-
-    loop(1, PILE, lambda r: fg_copy(r, pile_source(r) // 2, lax.rem(pile_source(r), 2)).wait_recv())
-    fg_in[z_lo, side] = fg[side, z_lo]
-    both = (fg_in[:, 0].astype(F32) + fg_in[:, 1].astype(F32)) * (1.0 / 512.0)
-    fg_own[0] = both[:, :8]
-    fg_own[1] = both[:, 8:]
-    fg_trade.start()
-    fg_trade.wait_recv()
-    mine, other = fg_own[core], fg_sib[...]
-    fg_rows[:, 0] = jnp.where(core == 0, mine, other)
-    fg_rows[:, 1] = jnp.where(core == 0, other, mine)
-    for b in range(N_DP):
-        for c in range(8):
-            fg_ref[b : b + 1, c * T : (c + 1) * T] = fg_rows[b // 2, b % 2, c : c + 1, :]
-
-    tap_trade.wait_send()
+    out_ref[...] = lo_in[...].reshape(BLK, BLK).T
+
+    pl.when(side == 1)(close_filter_grad)
     fg_trade.wait_send()
     for g in range(2):
-
-        def sent(i, g=g):
-            v_copy(g, i, yx).wait_send()
-            g_copy(g, i, yx).wait_send()
-            lo_copy(g, i, yx).wait_send()
-
-        loop(1, N_SLOT, sent)
-
-        def sent_over(i, g=g):
-            r_copy(g, i, yx).wait_send()
-            for h in range(2):
-                z_copy(g, h, i).wait_send()
-
-        loop(0, N_SLOT, sent_over)
-
-    def sent_column(r):
-        tap_copy(r, side, z_lo).wait_send()
-        fg_copy(r, z_lo, side).wait_send()
-
-    loop(1, PILE, sent_column)
+        for h in range(2):
+            for half in range(2):
+                z_copy(g, h, half).wait_send()
+    for g in range(2):
+        loop(1, N_SLOT, lambda i, g=g: lo_copy(g, i, yx).wait_send())
+    loop(1, PILE, lambda r: fg_copy(r, z_lo, side).wait_send())
 
 
 def shards(value, gate, grad_out, filter_taps, skip):
     taps = filter_taps[:, 0, :].T
     any_spec = pl.BlockSpec(memory_space=pl.ANY)
     vmem_spec = pl.BlockSpec(memory_space=pltpu.VMEM)
-    grad, fg = pl.pallas_call(
+    long_out, fg = pl.pallas_call(
         kernel,
         out_shape=(
             jax.ShapeDtypeStruct((BLK, BLK), BF16),
@@ -396,7 +400,7 @@
             pltpu.VMEM((2, BLK, BLK), BF16),
             pltpu.VMEM((2, HALF, BLK), F32),
             pltpu.VMEM((2, N_T + PAD + 1, T, T), F32),
-            pltpu.VMEM((N_T, 8, T), F32),
+            pltpu.VMEM((N_T, 16, T), F32),
             pltpu.VMEM((2, HALF, BLK), BF16),
             pltpu.VMEM((N_SLOT, 2, GROUP, BLK), BF16),
             pltpu.VMEM((2, 8, 16, T), BF16),
@@ -405,10 +409,10 @@
             pltpu.VMEM((8, 8, T), F32),
             pltpu.VMEM((8, 2, 8, T), F32),
             pltpu.SemaphoreType.DMA((5,)),
-            pltpu.SemaphoreType.DMA((2, 2, N_SLOT)),
-            pltpu.SemaphoreType.DMA((2, 2, N_SLOT)),
-            pltpu.SemaphoreType.DMA((2, 2, N_SLOT)),
-            pltpu.SemaphoreType.DMA((2, 2, 2, N_SLOT)),
+            pltpu.SemaphoreType.DMA((2, N_SLOT)),
+            pltpu.SemaphoreType.DMA((2, N_SLOT)),
+            pltpu.SemaphoreType.DMA((2, N_SLOT)),
+            pltpu.SemaphoreType.DMA((2, 2, 2, 2)),
             pltpu.SemaphoreType.DMA((2, PILE)),
             pltpu.SemaphoreType.DMA((2, 2, N_SLOT)),
             pltpu.SemaphoreType.DMA((2, PILE)),
@@ -420,6 +424,7 @@
         cost_estimate=pl.CostEstimate(flops=2 * 2**33, bytes_accessed=4 * 2**20, transcendentals=0),
         name="hyena",
     )(value, gate, grad_out, taps, skip[None, :])
+    grad = (long_out.astype(F32) * grad_out.astype(F32)).astype(BF16)
     return grad, fg.T[:, None, :]
 
 

time: 92.9 us -> 87.1 us (0.938)
  the two profiles are of different devices: /device:TPU:417 before, /device:TPU:8 now
where the time goes in v3:
time: 87.1 us; the launch traced here: 87 us
  Pallas kernels  83.7 us (96%)
  other arithmetic  2 us (2%)
    pallas_call x1, Pallas kernels, shards(): pl.pallas_call(kernel, out_shape=(jax.ShapeDtypeStruct((BLK, BLK), BF16),...  83.7 us
    convert_element_type x1, other arithmetic, shards(): grad = (long_out.astype(F32) * grad_out.astype(F32)).astype(BF16)  2 us

profile of v3, /device:TPU:8, one launch (start us, length us, event | category | flops | bytes accessed | tf_op | source)
XLA Modules:
  0.0 87.0 jit_solution(16599253970491925749)
XLA Ops:
  0.6 0.0 copy-start
  0.6 83.7 %hyena.1 = (bf16[512,512]{1,0:T(8,128)(2,1)}, f32[16,1024]{1,0:T(8,128)}) custom-call(bf16[512,512]{1,0:T(8,128)(2,1)} %value_hbm.1, bf16[512,512]{1,0:T(8,128)(2,1)} %gate_hbm.1, bf16[512,512]{1,0:T(8,128)(2,1)} %cot_hbm.1, f32[16,1024]{1,0:T(8,128)} %bitcast.8, f32[1,512]{1,0:T(1,128)} %bitcast.9), custom_call_target="tpu_custom_call" | custom-call | flops 17179869184 | bytes 4194304 | tf_op jit(solution)/shard_map/hyena/pallas_call | solution.py:376
  84.3 0.0 copy-done
  84.3 0.0 copy-start.1
  84.3 2.0 %multiply_convert_fusion = bf16[512,512]{1,0:T(8,128)(2,1)} fusion(bf16[512,512]{1,0:T(8,128)(2,1)S(1)} %copy-done, bf16[512,512]{1,0:T(8,128)(2,1)} %get-tuple-element.4), kind=kLoop, calls=%fused_computation | loop fusion | flops 1048576 | bytes 1572864 | tf_op jit(solution)/shard_map/convert_element_type | solution.py:427
  86.3 0.0 copy-done.1
  86.3 0.6 copy.8
Async XLA Ops:
  0.6 83.7 %copy-start = (bf16[512,512]{1,0:T(8,128)(2,1)S(1)}, bf16[512,512]{1,0:T(8,128)(2,1)}, u32[]{:S(2)}) copy-start(bf16[512,512]{1,0:T(8,128)(2,1)} %cot_hbm.1) | copy-start | bytes 1572868
  84.3 2.0 %copy-start.1 = (f32[16,1024]{1,0:T(8,128)S(1)}, f32[16,1024]{1,0:T(8,128)}, u32[]{:S(2)}) copy-start(f32[16,1024]{1,0:T(8,128)} %get-tuple-element.5) | copy-start | bytes 196612

commit v4 on v3

--- a/solution.py
+++ b/solution.py
@@ -116,6 +116,11 @@
     loads[3].wait()
     gloc[...] = (gat[...].astype(F32) * cot[...].astype(F32)).astype(BF16).T.reshape(N_SLOT, 2, GROUP, BLK)
 
+    @pl.when(side == 0)
+    def _():
+        for g in range(2):
+            vals[1, g, HALF - GROUP :] = jnp.zeros((GROUP, BLK), BF16)
+
     pl.semaphore_wait(barrier, PILE + 2 * (N_SLOT - 1))
 
     def r_copy(i, slot_at_receiver):
@@ -124,13 +129,31 @@
             r_sem.at[0, i], r_sem.at[1, i], device(z + way(yx, plane_peer(i)), plane_peer(i)),
         )
 
-    def z_copy(g, h, half):
-        rows = pl.ds(half * (HALF // 2), HALF // 2)
+    def z_copy(g, h, half, short=False):
+        rows = pl.ds(half * (HALF // 2), HALF // 2 - GROUP if short else HALF // 2)
         lanes = pl.ds(pl.multiple_of(h * HALF, HALF), HALF)
         return remote(
             relay.at[g, rows, lanes], vals.at[1, g, rows, lanes],
             z_sem.at[0, g, h, half], z_sem.at[1, g, h, half], device(z + 7 * way(8 * half, yx), yx),
         )
+
+    def z_each(g, h, half, to_side, act):
+        if half == 0:
+            act(z_copy(g, h, 0))
+        else:
+            pl.when(to_side == 0)(lambda: act(z_copy(g, h, 1, True)))
+            pl.when(to_side == 1)(lambda: act(z_copy(g, h, 1)))
+
+    late_side = lax.rem(z + 7 * way(8, yx) + 16, 16) // 8
+
+    def z_start(g, h, half):
+        z_each(g, h, half, late_side, lambda copy: copy.start())
+
+    def z_wait_send(g, h, half):
+        z_each(g, h, half, late_side, lambda copy: copy.wait_send())
+
+    def z_wait_recv(g, h, half):
+        z_each(g, h, half, side, lambda copy: copy.wait_recv())
 
     def v_copy(i, slot_at_receiver):
         return remote(
@@ -180,9 +203,9 @@
     for half in range(2):
         for n in range(8 * half, 8 * half + 8):
             r_copy(lax.rem(yx + N_SLOT - n, N_SLOT), n).wait_recv()
-        z_copy(0, 0, half).start()
+        z_start(0, 0, half)
     for half in range(2):
-        z_copy(0, 1, half).start()
+        z_start(0, 1, half)
 
     taps_in[side, z_lo] = tap_mix[z_lo]
     for g in range(2):
@@ -254,12 +277,18 @@
     def finish_conv(g):
         scale = skip_rows[pl.ds(pl.multiple_of((yx * 2 + g) * GROUP, GROUP), GROUP), :]
         scale = jnp.concatenate([scale] * 4, axis=1)
-        for n in range(N_SLOT):
-            wide = vals[0, g, n * GROUP : (n + 1) * GROUP, :].astype(F32)
-            rows = slice(n * GROUP, (n + 1) * GROUP)
-            lo[g, rows, :] = (acc[g, rows, :] * (1.0 / 128.0) + scale * wide).astype(BF16)
-        loop(1, N_SLOT, lambda i: lo_copy(g, i, yx).start())
-        lo_in[yx, g] = lo[g, rows_at(yx), :]
+
+        def piece(i):
+            rows = rows_at(plane_peer(i))
+            wide = vals[0, g, rows, :].astype(F32)
+            return (acc[g, rows, :] * (1.0 / 128.0) + scale * wide).astype(BF16)
+
+        def piece_out(i):
+            lo[g, rows_at(plane_peer(i)), :] = piece(i)
+            lo_copy(g, i, yx).start()
+
+        loop(1, N_SLOT, piece_out)
+        lo_in[yx, g] = piece(0)
 
     def finish_corr(g):
         def strip(d):
@@ -327,12 +356,12 @@
         h = lax.rem(n, 2)
         pl.when(n == 3)(sent)
         for half in range(2):
-            z_copy(g, h, half).wait_recv()
-
-        @pl.when(n == 0)
+            z_wait_recv(g, h, half)
+
+        @pl.when(g == 0)
         def _():
             for half in range(2):
-                z_copy(1, 0, half).start()
+                z_start(1, h, half)
 
         convolve(1, g, h, 1)
 
@@ -346,24 +375,18 @@
         def _():
             finish_corr(g)
 
-        @pl.when(n == 1)
-        def _():
-            for half in range(2):
-                z_copy(1, 1, half).start()
-
     loop(0, 4, phase)
-    pl.when(side == 0)(close_filter_grad)
 
     for g in range(2):
         loop(1, N_SLOT, lambda i, g=g: lo_copy(g, i, plane_source(i)).wait_recv())
     out_ref[...] = lo_in[...].reshape(BLK, BLK).T
 
-    pl.when(side == 1)(close_filter_grad)
+    close_filter_grad()
     fg_trade.wait_send()
     for g in range(2):
         for h in range(2):
             for half in range(2):
-                z_copy(g, h, half).wait_send()
+                z_wait_send(g, h, half)
     for g in range(2):
         loop(1, N_SLOT, lambda i, g=g: lo_copy(g, i, yx).wait_send())
     loop(1, PILE, lambda r: fg_copy(r, z_lo, side).wait_send())

time: 87.1 us -> 86.3 us (level)
  the two profiles are of different devices: /device:TPU:8 before, /device:TPU:33 now
where the time goes in v4:
time: 86.3 us; the launch traced here: 86.2 us
  Pallas kernels  82.9 us (96%)
  other arithmetic  2 us (2%)
    pallas_call x1, Pallas kernels, shards(): pl.pallas_call(kernel, out_shape=(jax.ShapeDtypeStruct((BLK, BLK), BF16),...  82.9 us
    convert_element_type x1, other arithmetic, shards(): grad = (long_out.astype(F32) * grad_out.astype(F32)).astype(BF16)  2 us

profile of v4, /device:TPU:33, one launch (start us, length us, event | category | flops | bytes accessed | tf_op | source)
XLA Modules:
  0.0 86.2 jit_solution(4736293459516618576)
XLA Ops:
  0.6 0.0 copy-start
  0.6 82.9 %hyena.1 = (bf16[512,512]{1,0:T(8,128)(2,1)}, f32[16,1024]{1,0:T(8,128)}) custom-call(bf16[512,512]{1,0:T(8,128)(2,1)} %value_hbm.1, bf16[512,512]{1,0:T(8,128)(2,1)} %gate_hbm.1, bf16[512,512]{1,0:T(8,128)(2,1)} %cot_hbm.1, f32[16,1024]{1,0:T(8,128)} %bitcast.8, f32[1,512]{1,0:T(1,128)} %bitcast.9), custom_call_target="tpu_custom_call" | custom-call | flops 17179869184 | bytes 4194304 | tf_op jit(solution)/shard_map/hyena/pallas_call | solution.py:399
  83.5 0.0 copy-done
  83.5 0.0 copy-start.1
  83.6 2.0 %multiply_convert_fusion = bf16[512,512]{1,0:T(8,128)(2,1)} fusion(bf16[512,512]{1,0:T(8,128)(2,1)S(1)} %copy-done, bf16[512,512]{1,0:T(8,128)(2,1)} %get-tuple-element.4), kind=kLoop, calls=%fused_computation | loop fusion | flops 1048576 | bytes 1572864 | tf_op jit(solution)/shard_map/convert_element_type | solution.py:450
  85.6 0.0 copy-done.1
  85.6 0.6 copy.8
Async XLA Ops:
  0.6 82.9 %copy-start = (bf16[512,512]{1,0:T(8,128)(2,1)S(1)}, bf16[512,512]{1,0:T(8,128)(2,1)}, u32[]{:S(2)}) copy-start(bf16[512,512]{1,0:T(8,128)(2,1)} %cot_hbm.1) | copy-start | bytes 1572868
  83.5 2.0 %copy-start.1 = (f32[16,1024]{1,0:T(8,128)S(1)}, f32[16,1024]{1,0:T(8,128)}, u32[]{:S(2)}) copy-start(f32[16,1024]{1,0:T(8,128)} %get-tuple-element.5) | copy-start | bytes 196612
